TPU v7x, 512 devices: a whole 4x8x8 slice. The times are simulated.
512 devices in a mesh: dp: 16 (over x, z_lo, core), ctx: 32 (over z_hi, y).
Axes of the slice: x: 4, y: 8, z: 8 (z_hi: 4, z_lo: 2; z = z_hi * 2 + z_lo), core: 2. Of those that a mesh axis runs over, the one named last changes fastest.
Arguments:
- queries: bfloat16 [16, 4096, 1024], P('dp', 'ctx'), may hold values from -60 to 60
- keys: bfloat16 [16, 4096, 128], P('dp', 'ctx'), may hold values from -6 to 6
- values: bfloat16 [16, 4096, 192], P('dp', 'ctx'), may hold values from -96 to 96
- features_fine: bfloat16 [16, 8192, 1536], P('dp', 'ctx'), may hold values from -6 to 6
- rc_state: bfloat16 [16, 4096, 1536], P('dp', 'ctx'), may hold values from -6 to 6
- conv_weight: float32 [5, 1536], replicated, may hold values from -2.5 to 2.5
Outputs:
- d_fine: bfloat16 [16, 8192, 1536], P('dp', 'ctx')
- d_weight: float32 [5, 1536], replicated
All inputs are finite; a program needn't handle non-finite values.
Results may differ from a plain program's by a relative error of at most 0.0085.
Values may be sent and summed in bfloat16 or wider, within the bound.
A program may use at most 64 MiB of HBM per device.

v0:
```python
import math
import jax
import jax.numpy as jnp
from jax import lax
from jax.sharding import PartitionSpec as P

HEADS = 8
KW = 5


def padded_2(cells, sides, width):
    for axis, dim in sides:
        count = lax.axis_size(axis)
        ends = count - 1
        head = lax.slice_in_dim(cells, 0, width, axis=dim)
        tail = lax.slice_in_dim(cells, cells.shape[dim] - width, cells.shape[dim], axis=dim)
        cells = jnp.concatenate(
            [
                lax.ppermute(tail, axis, [(i, (i + 1) % count) for i in range(ends)]),
                cells,
                lax.ppermute(head, axis, [((i + 1) % count, i) for i in range(ends)]),
            ],
            axis=dim,
        )
    return cells


def body(queries, keys, values, features_fine, rc_state, conv_weight):
    tok_rows = queries.shape[1]
    key_size = keys.shape[2]
    value_size = values.shape[2]
    q_heads = queries[0].reshape(tok_rows, HEADS, key_size)
    ctx_count = lax.axis_size("ctx")
    run_top = jnp.full((tok_rows, HEADS), -1e30, jnp.float32)
    key_piece = lax.all_gather(keys, "ctx", axis=1, tiled=True)
    value_piece = lax.all_gather(values, "ctx", axis=1, tiled=True)
    scores = jnp.einsum(
        "qhd,kd->qhk", q_heads, key_piece[0], preferred_element_type=jnp.float32
    ) * key_size ** (-0.5)
    new_top = jnp.maximum(run_top, jnp.max(scores, axis=-1))
    expd = jnp.exp(scores - new_top[..., None])
    new_total = jnp.sum(expd, axis=-1)
    mixed = jnp.einsum(
        "qhk,kv->qhv", expd.astype(jnp.bfloat16), value_piece[0], preferred_element_type=jnp.float32
    )
    attended = (mixed / new_total[..., None]).reshape(tok_rows, HEADS * value_size)[None]
    padded = padded_2(features_fine, (("ctx", 1),), 2)
    taps = [padded[:, k : k + 2 * tok_rows : 2, :].astype(jnp.float32) for k in range(KW)]
    coarse = conv_weight[0] * taps[0]
    for k in range(1, KW):
        coarse = coarse + conv_weight[k] * taps[k]
    slices = lax.all_to_all(rc_state, "ctx", split_axis=2, concat_axis=0, tiled=True)
    flipped = slices[::-1]
    mirrored = lax.all_to_all(flipped, "ctx", split_axis=0, concat_axis=2, tiled=True)
    grad = coarse + attended - mirrored[:, ::-1, :].astype(jnp.float32)
    gpad = padded_2(grad.astype(jnp.bfloat16), (("ctx", 1),), 1).astype(grad.dtype)
    even = (
        conv_weight[0] * gpad[:, 2:]
        + conv_weight[2] * gpad[:, 1:-1]
        + conv_weight[4] * gpad[:, :-2]
    )
    odd = conv_weight[1] * gpad[:, 2:] + conv_weight[3] * gpad[:, 1:-1]
    d_fine = (
        jnp.stack([even, odd], axis=2)
        .reshape(grad.shape[0], 2 * tok_rows, grad.shape[2])
        .astype(jnp.bfloat16)
    )
    partial_grad = jnp.stack([jnp.sum(grad * taps[k], axis=(0, 1)) for k in range(KW)])
    summed = lax.psum(partial_grad, ("dp", "ctx"))
    scale = 1.0 / math.sqrt(lax.axis_size("dp") * tok_rows * ctx_count)
    return (d_fine, summed * scale)


def solution(mesh):
    placed = (
        P("dp", "ctx", None),
        P("dp", "ctx", None),
        P("dp", "ctx", None),
        P("dp", "ctx", None),
        P("dp", "ctx", None),
        P(),
    )
    return jax.shard_map(
        body, mesh=mesh, in_specs=placed, out_specs=(P("dp", "ctx", None), P()), check_vma=False
    )
```

profile of v0, /device:TPU:184, one launch (start us, length us, event | category | flops | bytes accessed | tf_op | source)
XLA Modules:
  0.0 341.5 jit_solution(18383458230890813925)
XLA Ops:
  7.2 0.0 all-gather.3.cloned.1.call-start
  7.2 0.7 all-gather.3.cloned.1.call-update
  7.9 2.2 copy.29
  10.1 0.5 broadcast.15
  10.6 8.8 %reduce.10 = bf16[1536,128]{1,0:T(8,128)(2,1)S(1)} reduce(bf16[1536,1,128]{2,1,0:T(2,128)(2,1)S(1)} %bitcast.34, bf16[]{:T(256)} %broadcast.15), dimensions={1}, to_apply=%bitcast.29.reduce_sub_computation | reduce | bytes 786434
  19.4 0.8 reshape.84
  20.2 0.0 copy-start.1
  20.2 13.8 %all-to-all-start = ((bf16[32,2,3072]{2,1,0:T(2,128)(2,1)}), bf16[32,2,3072]{2,1,0:T(2,128)(2,1)S(1)}, u32[]{:S(2)}, u32[]{:S(2)}) async-start(bf16[32,2,3072]{2,1,0:T(2,128)(2,1)} %reshape.84), calls=%async_computation | async-start | bytes 786432 | tf_op jit(solution)/shard_map/all_to_all | solution.py:52
  34.0 0.0 all-gather.5.cloned.1.call-start
  34.1 0.7 all-gather.5.cloned.1.call-update
  34.8 0.0 copy-start.2
  34.8 12.8 %all-to-all-done = bf16[32,2,3072]{2,1,0:T(2,128)(2,1)S(1)} async-done(((bf16[32,2,3072]{2,1,0:T(2,128)(2,1)}), bf16[32,2,3072]{2,1,0:T(2,128)(2,1)S(1)}, u32[]{:S(2)}, u32[]{:S(2)}) %all-to-all-start) | async-done | bytes 393248 | tf_op jit(solution)/shard_map/all_to_all | solution.py:52
  47.6 0.3 reshape.85
  47.9 0.1 copy.31
  48.0 0.8 rev.6
  48.7 8.5 %all-to-all-start.1 = ((bf16[32,128,48]{1,2,0:T(8,128)(2,1)}), bf16[32,128,48]{1,2,0:T(8,128)(2,1)S(1)}, u32[]{:S(2)}, u32[]{:S(2)}) async-start(bf16[32,128,48]{1,2,0:T(8,128)(2,1)} %rev.6), calls=%async_computation.1 | async-start | bytes 786432 | tf_op jit(solution)/shard_map/all_to_all | solution.py:54
  57.2 0.0 copy-done.1
  57.3 0.3 copy.24
  57.5 5.5 %collective-permute-start = (bf16[1,2,1536]{1,2,0:T(8,128)(2,1)S(1)}, bf16[1,2,1536]{1,2,0:T(8,128)(2,1)}, u32[]{:S(2)}, u32[]{:S(2)}) collective-permute-start(bf16[1,2,1536]{1,2,0:T(8,128)(2,1)S(1)} %copy.24), channel_id=1, source_target_pairs={{0,1},{1,2},{2,3},{3,4},{4,5},{5,6},{6,7},{7,8},{8,9},{9,10},{10,1... | collective-permute-start | bytes 18440 | tf_op jit(solution)/shard_map/ppermute | solution.py:19
  63.0 0.3 copy.25
  63.3 2.1 collective-permute-start.1
  65.4 0.0 copy-done.2
  65.4 0.1 slice_reduce_fusion.4
  65.5 0.3 copy.26
  65.8 1.0 copy.32
  66.8 14.4 %slice.65 = bf16[1,128,1536]{1,2,0:T(8,128)(2,1)S(1)} slice(bf16[1,256,1536]{1,2,0:T(8,128)(2,1)S(1)} %copy.26), slice={[0:1:1], [0:256:2], [0:1536:1]} | slice | bytes 786432 | tf_op jit(solution)/shard_map/slice | solution.py:48
  81.2 0.0 collective-permute-done
  81.2 5.9 %collective-permute-done.1 = bf16[1,2,1536]{1,2,0:T(8,128)(2,1)} collective-permute-done((bf16[1,2,1536]{1,2,0:T(8,128)(2,1)S(1)}, bf16[1,2,1536]{1,2,0:T(8,128)(2,1)}, u32[]{:S(2)}, u32[]{:S(2)}) %collective-permute-start.1) | collective-permute-done | bytes 6176 | tf_op jit(solution)/shard_map/ppermute | solution.py:21
  87.1 1.8 pad_maximum_fusion
  88.9 14.4 %slice.61 = bf16[1,128,1536]{1,2,0:T(8,128)(2,1)S(1)} slice(bf16[1,260,1536]{1,2,0:T(8,128)(2,1)S(1)} %pad_maximum_fusion), slice={[0:1:1], [0:256:2], [0:1536:1]} | slice | bytes 786432 | tf_op jit(solution)/shard_map/slice | solution.py:48
  103.3 14.4 %slice.63 = bf16[1,128,1536]{1,2,0:T(8,128)(2,1)S(1)} slice(bf16[1,260,1536]{1,2,0:T(8,128)(2,1)S(1)} %pad_maximum_fusion), slice={[0:1:1], [1:257:2], [0:1536:1]} | slice | bytes 786432 | tf_op jit(solution)/shard_map/slice | solution.py:48
  117.7 14.7 %slice.67 = bf16[1,128,1536]{1,2,0:T(8,128)(2,1)S(1)} slice(bf16[1,260,1536]{1,2,0:T(8,128)(2,1)S(1)} %pad_maximum_fusion), slice={[0:1:1], [3:259:2], [0:1536:1]} | slice | bytes 786432 | tf_op jit(solution)/shard_map/slice | solution.py:48
  132.4 15.0 %slice.69 = bf16[1,128,1536]{1,2,0:T(8,128)(2,1)} slice(bf16[1,260,1536]{1,2,0:T(8,128)(2,1)S(1)} %pad_maximum_fusion), slice={[0:1:1], [4:260:2], [0:1536:1]} | slice | bytes 786432 | tf_op jit(solution)/shard_map/slice | solution.py:48
  147.4 0.0 all-to-all-done.1
  147.4 1.3 rev.7
  148.7 0.0 all-gather.3.cloned.1.call-done
  148.8 9.3 %multiply_reduce_fusion = (f32[128,8]{0,1:T(8,128)S(1)}, f32[128,8,4096]{2,0,1:T(8,128)}) fusion(bf16[1,4096,128]{2,1,0:T(8,128)(2,1)} %all-gather.3.cloned.1.call-done, bf16[128,8,128]{2,1,0:T(8,128)(2,1)S(1)} %bitcast.36), kind=kOutput, calls=%fused_computation.1 | convolution fusion | flops 1082129408 | bytes 18092032 | tf_op jit(solution)/shard_map/qhd,kd->qhk/dot_general | solution.py:37
  158.0 8.6 %fusion = f32[128,8]{0,1:T(8,128)S(1)} fusion(f32[128,8,4096]{2,0,1:T(8,128)} %get-tuple-element.20, f32[128,8]{0,1:T(8,128)S(1)} %broadcast_maximum_fusion), kind=kLoop, calls=%fused_computation.2 | loop fusion | flops 12581888 | bytes 16785408 | tf_op jit(solution)/shard_map/reduce_sum | solution.py:42
  166.7 0.0 copy-start
  166.7 29.0 %all-gather.5.cloned.1.call-done = bf16[1,4096,192]{1,2,0:T(8,128)(2,1)} async-done(((bf16[1,128,192]{1,2,0:T(8,128)(2,1)}), bf16[1,4096,192]{1,2,0:T(8,128)(2,1)}) %all-gather.5.cloned.1.call-update) | async-done | bytes 1572880 | tf_op jit(solution)/shard_map/all_gather | solution.py:36
  195.6 8.0 %fusion.7 = f32[128,8,192]{0,2,1:T(8,128)S(1)} fusion(bf16[1,4096,192]{1,2,0:T(8,128)(2,1)} %all-gather.5.cloned.1.call-done, f32[128,8,4096]{2,0,1:T(8,128)} %get-tuple-element.20, f32[128,8]{0,1:T(8,128)S(1)} %broadcast_maximum_fusion, f32[128,8]{0,1:T(8,128)S(1)} %fusion), kind=kOutput, calls=%fused_computation.19 | convolution fusion | flops 1623392256 | bytes 19144704 | tf_op jit(solution)/shard_map/qhk,kv->qhv/dot_general | solution.py:43
  203.6 0.0 copy-done
  203.6 2.7 fusion.22
  206.4 0.1 stack.38
  206.5 93.2 %psum.7 = f32[5,1536]{1,0:T(8,128)S(1)} all-reduce(f32[5,1536]{1,0:T(8,128)S(1)} %stack.38), channel_id=1, replica_groups=mesh['dp'=16,'ctx'=32] {'dp','ctx'}, use_global_device_ids=true, to_apply=%region_7.0 | all-reduce | flops 7680 | bytes 61440 | tf_op jit(solution)/shard_map/psum | solution.py:69
  299.7 0.2 fusion.31
  299.9 6.2 %collective-permute-start.2 = (bf16[1,1,1536]{1,2,0:T(8,128)(2,1)S(1)}, bf16[1,1,1536]{1,2,0:T(8,128)(2,1)S(1)}, u32[]{:S(2)}, u32[]{:S(2)}) collective-permute-start(bf16[1,1,1536]{1,2,0:T(8,128)(2,1)S(1)} %get-tuple-element.17), channel_id=1, source_target_pairs={{0,1},{1,2},{2,3},{3,4},{4,5},{5,6},{6,7},{7,8},{8,9},{9,10},{10,1... | collective-permute-start | bytes 9224 | tf_op jit(solution)/shard_map/ppermute | solution.py:19
  306.1 1.9 collective-permute-start.3
  308.0 0.6 broadcast_multiply_fusion
  308.6 11.6 %collective-permute-done.2 = bf16[1,1,1536]{1,2,0:T(8,128)(2,1)S(1)} collective-permute-done((bf16[1,1,1536]{1,2,0:T(8,128)(2,1)S(1)}, bf16[1,1,1536]{1,2,0:T(8,128)(2,1)S(1)}, u32[]{:S(2)}, u32[]{:S(2)}) %collective-permute-start.2) | collective-permute-done | bytes 3104 | tf_op jit(solution)/shard_map/ppermute | solution.py:19
  320.2 10.3 %collective-permute-done.3 = bf16[1,1,1536]{1,2,0:T(8,128)(2,1)S(1)} collective-permute-done((bf16[1,1,1536]{1,2,0:T(8,128)(2,1)S(1)}, bf16[1,1,1536]{1,2,0:T(8,128)(2,1)S(1)}, u32[]{:S(2)}, u32[]{:S(2)}) %collective-permute-start.3) | collective-permute-done | bytes 3104 | tf_op jit(solution)/shard_map/ppermute | solution.py:21
  330.5 0.4 maximum_convert_fusion
  330.9 1.7 fusion.26
  332.6 0.1 pad_maximum_fusion.1
  332.7 0.8 copy.30
  333.5 1.2 convert_element_type.56
  (7 shorter events, 0.0 us)
Async XLA Ops:
  7.2 141.6 %all-gather.3.cloned.1.call-start = ((), (), s32[]{:S(2)}) async-start(), calls=%async_computation.2 | async-start | bytes 1081344 | tf_op jit(solution)/shard_map/all_gather | solution.py:35
  20.2 37.0 %copy-start.1 = (bf16[1,256,1536]{2,1,0:T(8,128)(2,1)S(1)}, bf16[1,256,1536]{2,1,0:T(8,128)(2,1)}, u32[]{:S(2)}) copy-start(bf16[1,256,1536]{2,1,0:T(8,128)(2,1)} %param.9) | copy-start | bytes 2359300
  20.2 27.4 %all-to-all-start = ((bf16[32,2,3072]{2,1,0:T(2,128)(2,1)}), bf16[32,2,3072]{2,1,0:T(2,128)(2,1)S(1)}, u32[]{:S(2)}, u32[]{:S(2)}) async-start(bf16[32,2,3072]{2,1,0:T(2,128)(2,1)} %reshape.84), calls=%async_computation | async-start | bytes 786432 | tf_op jit(solution)/shard_map/all_to_all | solution.py:52
  34.0 161.6 %all-gather.5.cloned.1.call-start = ((), (), s32[]{:S(2)}) async-start(), calls=%async_computation.3 | async-start | bytes 1622016 | tf_op jit(solution)/shard_map/all_gather | solution.py:36
  34.8 30.6 %copy-start.2 = (f32[5,1536]{1,0:T(8,128)S(1)}, f32[5,1536]{1,0:T(8,128)}, u32[]{:S(2)}) copy-start(f32[5,1536]{1,0:T(8,128)} %param.11) | copy-start | bytes 92164
  48.7 98.6 %all-to-all-start.1 = ((bf16[32,128,48]{1,2,0:T(8,128)(2,1)}), bf16[32,128,48]{1,2,0:T(8,128)(2,1)S(1)}, u32[]{:S(2)}, u32[]{:S(2)}) async-start(bf16[32,128,48]{1,2,0:T(8,128)(2,1)} %rev.6), calls=%async_computation.1 | async-start | bytes 786432 | tf_op jit(solution)/shard_map/all_to_all | solution.py:54
  57.5 23.6 %collective-permute-start = (bf16[1,2,1536]{1,2,0:T(8,128)(2,1)S(1)}, bf16[1,2,1536]{1,2,0:T(8,128)(2,1)}, u32[]{:S(2)}, u32[]{:S(2)}) collective-permute-start(bf16[1,2,1536]{1,2,0:T(8,128)(2,1)S(1)} %copy.24), channel_id=1, source_target_pairs={{0,1},{1,2},{2,3},{3,4},{4,5},{5,6},{6,7},{7,8},{8,9},{9,10},{10,1... | collective-permute-start | bytes 18440 | tf_op jit(solution)/shard_map/ppermute | solution.py:19
  63.3 23.8 %collective-permute-start.1 = (bf16[1,2,1536]{1,2,0:T(8,128)(2,1)S(1)}, bf16[1,2,1536]{1,2,0:T(8,128)(2,1)}, u32[]{:S(2)}, u32[]{:S(2)}) collective-permute-start(bf16[1,2,1536]{1,2,0:T(8,128)(2,1)S(1)} %copy.25), channel_id=1, source_target_pairs={{1,0},{2,1},{3,2},{4,3},{5,4},{6,5},{7,6},{8,7},{9,8},{10,9},{11,1... | collective-permute-start | bytes 18440 | tf_op jit(solution)/shard_map/ppermute | solution.py:21
  166.7 36.9 %copy-start = (bf16[1,128,1536]{1,2,0:T(8,128)(2,1)S(1)}, bf16[1,128,1536]{1,2,0:T(8,128)(2,1)}, u32[]{:S(2)}) copy-start(bf16[1,128,1536]{1,2,0:T(8,128)(2,1)} %slice.69) | copy-start | bytes 1179652
  299.9 20.3 %collective-permute-start.2 = (bf16[1,1,1536]{1,2,0:T(8,128)(2,1)S(1)}, bf16[1,1,1536]{1,2,0:T(8,128)(2,1)S(1)}, u32[]{:S(2)}, u32[]{:S(2)}) collective-permute-start(bf16[1,1,1536]{1,2,0:T(8,128)(2,1)S(1)} %get-tuple-element.17), channel_id=1, source_target_pairs={{0,1},{1,2},{2,3},{3,4},{4,5},{5,6},{6,7},{7,8},{8,9},{9,10},{10,1... | collective-permute-start | bytes 9224 | tf_op jit(solution)/shard_map/ppermute | solution.py:19
  306.1 24.4 %collective-permute-start.3 = (bf16[1,1,1536]{1,2,0:T(8,128)(2,1)S(1)}, bf16[1,1,1536]{1,2,0:T(8,128)(2,1)S(1)}, u32[]{:S(2)}, u32[]{:S(2)}) collective-permute-start(bf16[1,1,1536]{1,2,0:T(8,128)(2,1)S(1)} %get-tuple-element.18), channel_id=1, source_target_pairs={{1,0},{2,1},{3,2},{4,3},{5,4},{6,5},{7,6},{8,7},{9,8},{10,9},{11,1... | collective-permute-start | bytes 9224 | tf_op jit(solution)/shard_map/ppermute | solution.py:21
Sparse Core Ops, SparseCore 0:
  11.2 102.2 all-gather.2
  116.5 79.0 all-gather.4
where the time goes:
time: 342 us; the launch traced here: 341 us
  blocking collectives  93.2 us (27%)
  local copies, waits for them, and re-layouts  82.9 us (24%)
  waiting for transfers between devices  70.9 us (21%)
  starting transfers between devices  38.1 us (11%)
  other arithmetic  24.9 us (7%)
  matrix products  17.2 us (5%)
  between operations  14.3 us (4%)
    psum x1, blocking collectives, body(): summed = lax.psum(partial_grad, ('dp', 'ctx'))  93.2 us
    slice x5, local copies, waits for them, and re-layouts, body(): padded[:, k:k + 2 * tok_rows:2, :].astype(jnp.float32)  72.8 us
    all_gather x1, waiting for transfers between devices, body(): value_piece = lax.all_gather(values, 'ctx', axis=1, tiled=True)  29 us
    ppermute x2, waiting for transfers between devices, padded_2(): lax.ppermute(head, axis, [((i + 1) % count, i) for i in range(ends)])  16.2 us
    all_to_all x1, starting transfers between devices, body(): lax.all_to_all(rc_state, 'ctx', split_axis=2, concat_axis=0, tiled=True)  13.8 us
    all_to_all x1, waiting for transfers between devices, body(): lax.all_to_all(rc_state, 'ctx', split_axis=2, concat_axis=0, tiled=True)  12.8 us
    ppermute x2, starting transfers between devices, padded_2(): lax.ppermute(tail, axis, [(i, (i + 1) % count) for i in range(ends)])  11.7 us
    ppermute x2, waiting for transfers between devices, padded_2(): lax.ppermute(tail, axis, [(i, (i + 1) % count) for i in range(ends)])  11.6 us
  transfers between devices with their start and end apart: 8, of which 5 were waited for; matrix products, arithmetic and copies ran while one was open for 32% of the time, Pallas kernels for 0%

commit v1 on v0

--- a/solution.py
+++ b/solution.py
@@ -66,7 +66,7 @@
         .astype(jnp.bfloat16)
     )
     partial_grad = jnp.stack([jnp.sum(grad * taps[k], axis=(0, 1)) for k in range(KW)])
-    summed = lax.psum(partial_grad, ("dp", "ctx"))
+    summed = lax.psum(lax.psum(partial_grad, "ctx"), "dp")
     scale = 1.0 / math.sqrt(lax.axis_size("dp") * tok_rows * ctx_count)
     return (d_fine, summed * scale)
 

time: 342 us -> 452 us (1.32)
  blocking collectives: 93.2 us -> 205 us
    psum x1 -> x2, blocking collectives: 93.2 us -> 205 us  [body(): summed = lax.psum(lax.psum(partial_grad, 'ctx'), 'dp')]
    ppermute x2, waiting for transfers between devices: 11.6 us -> 6.55 us  [padded_2(): lax.ppermute(tail, axis, [(i, (i + 1) % count) for i in range(ends)])]
  transfers between devices with their start and end apart: 8 -> 8, of which waited for: 5 -> 5; matrix products, arithmetic and copies ran while one was open for 32% -> 24% of each run, Pallas kernels for 0% -> 0%
where the time goes in v1:
time: 452 us; the launch traced here: 451 us
  blocking collectives  205 us (45%)
  local copies, waits for them, and re-layouts  82.9 us (18%)
  waiting for transfers between devices  66.5 us (15%)
  starting transfers between devices  40.3 us (9%)
  other arithmetic  24.9 us (6%)
  matrix products  17.2 us (4%)
  between operations  14.3 us (3%)
    psum x2, blocking collectives, body(): summed = lax.psum(lax.psum(partial_grad, 'ctx'), 'dp')  205 us
    slice x5, local copies, waits for them, and re-layouts, body(): padded[:, k:k + 2 * tok_rows:2, :].astype(jnp.float32)  72.8 us
    all_gather x1, waiting for transfers between devices, body(): value_piece = lax.all_gather(values, 'ctx', axis=1, tiled=True)  29 us
    ppermute x2, waiting for transfers between devices, padded_2(): lax.ppermute(head, axis, [((i + 1) % count, i) for i in range(ends)])  16.7 us
    ppermute x2, starting transfers between devices, padded_2(): lax.ppermute(tail, axis, [(i, (i + 1) % count) for i in range(ends)])  13.9 us
    all_to_all x1, starting transfers between devices, body(): lax.all_to_all(rc_state, 'ctx', split_axis=2, concat_axis=0, tiled=True)  13.8 us
    all_to_all x1, waiting for transfers between devices, body(): lax.all_to_all(rc_state, 'ctx', split_axis=2, concat_axis=0, tiled=True)  12.8 us
    dot_general x1, matrix products, body(): jnp.einsum('qhd,kd->qhk', q_heads, key_piece[0], preferred_element_type=j...  9.28 us
  transfers between devices with their start and end apart: 8, of which 5 were waited for; matrix products, arithmetic and copies ran while one was open for 24% of the time, Pallas kernels for 0%

profile of v1, /device:TPU:184, one launch (start us, length us, event | category | flops | bytes accessed | tf_op | source)
XLA Modules:
  0.0 451.0 jit_solution(5041187814327625734)
XLA Ops:
  7.2 0.0 all-gather.3.cloned.1.call-start
  7.2 0.7 all-gather.3.cloned.1.call-update
  7.9 2.2 copy.29
  10.1 0.5 broadcast.15
  10.6 8.8 %reduce.10 = bf16[1536,128]{1,0:T(8,128)(2,1)S(1)} reduce(bf16[1536,1,128]{2,1,0:T(2,128)(2,1)S(1)} %bitcast.34, bf16[]{:T(256)} %broadcast.15), dimensions={1}, to_apply=%bitcast.29.reduce_sub_computation | reduce | bytes 786434
  19.4 0.8 reshape.84
  20.2 0.0 copy-start.1
  20.2 13.8 %all-to-all-start = ((bf16[32,2,3072]{2,1,0:T(2,128)(2,1)}), bf16[32,2,3072]{2,1,0:T(2,128)(2,1)S(1)}, u32[]{:S(2)}, u32[]{:S(2)}) async-start(bf16[32,2,3072]{2,1,0:T(2,128)(2,1)} %reshape.84), calls=%async_computation | async-start | bytes 786432 | tf_op jit(solution)/shard_map/all_to_all | solution.py:52
  34.0 0.0 all-gather.5.cloned.1.call-start
  34.1 0.7 all-gather.5.cloned.1.call-update
  34.8 0.0 copy-start.2
  34.8 12.8 %all-to-all-done = bf16[32,2,3072]{2,1,0:T(2,128)(2,1)S(1)} async-done(((bf16[32,2,3072]{2,1,0:T(2,128)(2,1)}), bf16[32,2,3072]{2,1,0:T(2,128)(2,1)S(1)}, u32[]{:S(2)}, u32[]{:S(2)}) %all-to-all-start) | async-done | bytes 393248 | tf_op jit(solution)/shard_map/all_to_all | solution.py:52
  47.6 0.3 reshape.85
  47.9 0.1 copy.31
  48.0 0.8 rev.6
  48.7 8.5 %all-to-all-start.1 = ((bf16[32,128,48]{1,2,0:T(8,128)(2,1)}), bf16[32,128,48]{1,2,0:T(8,128)(2,1)S(1)}, u32[]{:S(2)}, u32[]{:S(2)}) async-start(bf16[32,128,48]{1,2,0:T(8,128)(2,1)} %rev.6), calls=%async_computation.1 | async-start | bytes 786432 | tf_op jit(solution)/shard_map/all_to_all | solution.py:54
  57.2 0.0 copy-done.1
  57.3 0.3 copy.24
  57.5 5.5 %collective-permute-start = (bf16[1,2,1536]{1,2,0:T(8,128)(2,1)S(1)}, bf16[1,2,1536]{1,2,0:T(8,128)(2,1)}, u32[]{:S(2)}, u32[]{:S(2)}) collective-permute-start(bf16[1,2,1536]{1,2,0:T(8,128)(2,1)S(1)} %copy.24), channel_id=1, source_target_pairs={{0,1},{1,2},{2,3},{3,4},{4,5},{5,6},{6,7},{7,8},{8,9},{9,10},{10,1... | collective-permute-start | bytes 18440 | tf_op jit(solution)/shard_map/ppermute | solution.py:19
  63.0 0.3 copy.25
  63.3 2.1 collective-permute-start.1
  65.4 0.0 copy-done.2
  65.4 0.1 slice_reduce_fusion.4
  65.5 0.3 copy.26
  65.8 1.0 copy.32
  66.8 14.4 %slice.65 = bf16[1,128,1536]{1,2,0:T(8,128)(2,1)S(1)} slice(bf16[1,256,1536]{1,2,0:T(8,128)(2,1)S(1)} %copy.26), slice={[0:1:1], [0:256:2], [0:1536:1]} | slice | bytes 786432 | tf_op jit(solution)/shard_map/slice | solution.py:48
  81.2 0.0 collective-permute-done
  81.2 5.9 %collective-permute-done.1 = bf16[1,2,1536]{1,2,0:T(8,128)(2,1)} collective-permute-done((bf16[1,2,1536]{1,2,0:T(8,128)(2,1)S(1)}, bf16[1,2,1536]{1,2,0:T(8,128)(2,1)}, u32[]{:S(2)}, u32[]{:S(2)}) %collective-permute-start.1) | collective-permute-done | bytes 6176 | tf_op jit(solution)/shard_map/ppermute | solution.py:21
  87.1 1.8 pad_maximum_fusion
  88.9 14.4 %slice.61 = bf16[1,128,1536]{1,2,0:T(8,128)(2,1)S(1)} slice(bf16[1,260,1536]{1,2,0:T(8,128)(2,1)S(1)} %pad_maximum_fusion), slice={[0:1:1], [0:256:2], [0:1536:1]} | slice | bytes 786432 | tf_op jit(solution)/shard_map/slice | solution.py:48
  103.3 14.4 %slice.63 = bf16[1,128,1536]{1,2,0:T(8,128)(2,1)S(1)} slice(bf16[1,260,1536]{1,2,0:T(8,128)(2,1)S(1)} %pad_maximum_fusion), slice={[0:1:1], [1:257:2], [0:1536:1]} | slice | bytes 786432 | tf_op jit(solution)/shard_map/slice | solution.py:48
  117.7 14.7 %slice.67 = bf16[1,128,1536]{1,2,0:T(8,128)(2,1)S(1)} slice(bf16[1,260,1536]{1,2,0:T(8,128)(2,1)S(1)} %pad_maximum_fusion), slice={[0:1:1], [3:259:2], [0:1536:1]} | slice | bytes 786432 | tf_op jit(solution)/shard_map/slice | solution.py:48
  132.4 15.0 %slice.69 = bf16[1,128,1536]{1,2,0:T(8,128)(2,1)} slice(bf16[1,260,1536]{1,2,0:T(8,128)(2,1)S(1)} %pad_maximum_fusion), slice={[0:1:1], [4:260:2], [0:1536:1]} | slice | bytes 786432 | tf_op jit(solution)/shard_map/slice | solution.py:48
  147.4 0.0 all-to-all-done.1
  147.4 1.3 rev.7
  148.7 0.0 all-gather.3.cloned.1.call-done
  148.8 9.3 %multiply_reduce_fusion = (f32[128,8]{0,1:T(8,128)S(1)}, f32[128,8,4096]{2,0,1:T(8,128)}) fusion(bf16[1,4096,128]{2,1,0:T(8,128)(2,1)} %all-gather.3.cloned.1.call-done, bf16[128,8,128]{2,1,0:T(8,128)(2,1)S(1)} %bitcast.36), kind=kOutput, calls=%fused_computation.1 | convolution fusion | flops 1082129408 | bytes 18092032 | tf_op jit(solution)/shard_map/qhd,kd->qhk/dot_general | solution.py:37
  158.0 8.6 %fusion = f32[128,8]{0,1:T(8,128)S(1)} fusion(f32[128,8,4096]{2,0,1:T(8,128)} %get-tuple-element.20, f32[128,8]{0,1:T(8,128)S(1)} %broadcast_maximum_fusion), kind=kLoop, calls=%fused_computation.2 | loop fusion | flops 12581888 | bytes 16785408 | tf_op jit(solution)/shard_map/reduce_sum | solution.py:42
  166.7 0.0 copy-start
  166.7 29.0 %all-gather.5.cloned.1.call-done = bf16[1,4096,192]{1,2,0:T(8,128)(2,1)} async-done(((bf16[1,128,192]{1,2,0:T(8,128)(2,1)}), bf16[1,4096,192]{1,2,0:T(8,128)(2,1)}) %all-gather.5.cloned.1.call-update) | async-done | bytes 1572880 | tf_op jit(solution)/shard_map/all_gather | solution.py:36
  195.6 8.0 %fusion.7 = f32[128,8,192]{0,2,1:T(8,128)S(1)} fusion(bf16[1,4096,192]{1,2,0:T(8,128)(2,1)} %all-gather.5.cloned.1.call-done, f32[128,8,4096]{2,0,1:T(8,128)} %get-tuple-element.20, f32[128,8]{0,1:T(8,128)S(1)} %broadcast_maximum_fusion, f32[128,8]{0,1:T(8,128)S(1)} %fusion), kind=kOutput, calls=%fused_computation.19 | convolution fusion | flops 1623392256 | bytes 19144704 | tf_op jit(solution)/shard_map/qhk,kv->qhv/dot_general | solution.py:43
  203.6 0.0 copy-done
  203.6 2.7 fusion.22
  206.4 0.1 stack.38
  206.5 152.0 %psum.14 = f32[5,1536]{1,0:T(8,128)S(1)} all-reduce(f32[5,1536]{1,0:T(8,128)S(1)} %stack.38), channel_id=1, replica_groups=mesh['dp'=16,'ctx'=32] {'ctx'}, use_global_device_ids=true, to_apply=%region_7.0 | all-reduce | flops 7680 | bytes 61440 | tf_op jit(solution)/shard_map/psum | solution.py:69
  358.5 53.0 %psum.15 = f32[5,1536]{1,0:T(8,128)S(1)} all-reduce(f32[5,1536]{1,0:T(8,128)S(1)} %psum.14), channel_id=1, replica_groups=mesh['dp'=16,'ctx'=32] {'dp'}, use_global_device_ids=true, to_apply=%region_8.0 | all-reduce | flops 7680 | bytes 61440 | tf_op jit(solution)/shard_map/psum | solution.py:69
  411.5 0.2 fusion.31
  411.6 8.4 %collective-permute-start.2 = (bf16[1,1,1536]{1,2,0:T(8,128)(2,1)S(1)}, bf16[1,1,1536]{1,2,0:T(8,128)(2,1)S(1)}, u32[]{:S(2)}, u32[]{:S(2)}) collective-permute-start(bf16[1,1,1536]{1,2,0:T(8,128)(2,1)S(1)} %get-tuple-element.17), channel_id=1, source_target_pairs={{0,1},{1,2},{2,3},{3,4},{4,5},{5,6},{6,7},{7,8},{8,9},{9,10},{10,1... | collective-permute-start | bytes 9224 | tf_op jit(solution)/shard_map/ppermute | solution.py:19
  420.1 1.9 collective-permute-start.3
  422.0 0.6 broadcast_multiply_fusion
  422.6 6.5 %collective-permute-done.2 = bf16[1,1,1536]{1,2,0:T(8,128)(2,1)S(1)} collective-permute-done((bf16[1,1,1536]{1,2,0:T(8,128)(2,1)S(1)}, bf16[1,1,1536]{1,2,0:T(8,128)(2,1)S(1)}, u32[]{:S(2)}, u32[]{:S(2)}) %collective-permute-start.2) | collective-permute-done | bytes 3104 | tf_op jit(solution)/shard_map/ppermute | solution.py:19
  429.2 10.9 %collective-permute-done.3 = bf16[1,1,1536]{1,2,0:T(8,128)(2,1)S(1)} collective-permute-done((bf16[1,1,1536]{1,2,0:T(8,128)(2,1)S(1)}, bf16[1,1,1536]{1,2,0:T(8,128)(2,1)S(1)}, u32[]{:S(2)}, u32[]{:S(2)}) %collective-permute-start.3) | collective-permute-done | bytes 3104 | tf_op jit(solution)/shard_map/ppermute | solution.py:21
  440.0 0.4 maximum_convert_fusion
  440.5 1.7 fusion.26
  442.2 0.1 pad_maximum_fusion.1
  442.3 0.8 copy.30
  443.0 1.2 convert_element_type.56
  (7 shorter events, 0.0 us)
Async XLA Ops:
  7.2 141.6 %all-gather.3.cloned.1.call-start = ((), (), s32[]{:S(2)}) async-start(), calls=%async_computation.2 | async-start | bytes 1081344 | tf_op jit(solution)/shard_map/all_gather | solution.py:35
  20.2 37.0 %copy-start.1 = (bf16[1,256,1536]{2,1,0:T(8,128)(2,1)S(1)}, bf16[1,256,1536]{2,1,0:T(8,128)(2,1)}, u32[]{:S(2)}) copy-start(bf16[1,256,1536]{2,1,0:T(8,128)(2,1)} %param.9) | copy-start | bytes 2359300
  20.2 27.4 %all-to-all-start = ((bf16[32,2,3072]{2,1,0:T(2,128)(2,1)}), bf16[32,2,3072]{2,1,0:T(2,128)(2,1)S(1)}, u32[]{:S(2)}, u32[]{:S(2)}) async-start(bf16[32,2,3072]{2,1,0:T(2,128)(2,1)} %reshape.84), calls=%async_computation | async-start | bytes 786432 | tf_op jit(solution)/shard_map/all_to_all | solution.py:52
  34.0 161.6 %all-gather.5.cloned.1.call-start = ((), (), s32[]{:S(2)}) async-start(), calls=%async_computation.3 | async-start | bytes 1622016 | tf_op jit(solution)/shard_map/all_gather | solution.py:36
  34.8 30.6 %copy-start.2 = (f32[5,1536]{1,0:T(8,128)S(1)}, f32[5,1536]{1,0:T(8,128)}, u32[]{:S(2)}) copy-start(f32[5,1536]{1,0:T(8,128)} %param.11) | copy-start | bytes 92164
  48.7 98.6 %all-to-all-start.1 = ((bf16[32,128,48]{1,2,0:T(8,128)(2,1)}), bf16[32,128,48]{1,2,0:T(8,128)(2,1)S(1)}, u32[]{:S(2)}, u32[]{:S(2)}) async-start(bf16[32,128,48]{1,2,0:T(8,128)(2,1)} %rev.6), calls=%async_computation.1 | async-start | bytes 786432 | tf_op jit(solution)/shard_map/all_to_all | solution.py:54
  57.5 23.6 %collective-permute-start = (bf16[1,2,1536]{1,2,0:T(8,128)(2,1)S(1)}, bf16[1,2,1536]{1,2,0:T(8,128)(2,1)}, u32[]{:S(2)}, u32[]{:S(2)}) collective-permute-start(bf16[1,2,1536]{1,2,0:T(8,128)(2,1)S(1)} %copy.24), channel_id=1, source_target_pairs={{0,1},{1,2},{2,3},{3,4},{4,5},{5,6},{6,7},{7,8},{8,9},{9,10},{10,1... | collective-permute-start | bytes 18440 | tf_op jit(solution)/shard_map/ppermute | solution.py:19
  63.3 23.8 %collective-permute-start.1 = (bf16[1,2,1536]{1,2,0:T(8,128)(2,1)S(1)}, bf16[1,2,1536]{1,2,0:T(8,128)(2,1)}, u32[]{:S(2)}, u32[]{:S(2)}) collective-permute-start(bf16[1,2,1536]{1,2,0:T(8,128)(2,1)S(1)} %copy.25), channel_id=1, source_target_pairs={{1,0},{2,1},{3,2},{4,3},{5,4},{6,5},{7,6},{8,7},{9,8},{10,9},{11,1... | collective-permute-start | bytes 18440 | tf_op jit(solution)/shard_map/ppermute | solution.py:21
  166.7 36.9 %copy-start = (bf16[1,128,1536]{1,2,0:T(8,128)(2,1)S(1)}, bf16[1,128,1536]{1,2,0:T(8,128)(2,1)}, u32[]{:S(2)}) copy-start(bf16[1,128,1536]{1,2,0:T(8,128)(2,1)} %slice.69) | copy-start | bytes 1179652
  411.6 17.6 %collective-permute-start.2 = (bf16[1,1,1536]{1,2,0:T(8,128)(2,1)S(1)}, bf16[1,1,1536]{1,2,0:T(8,128)(2,1)S(1)}, u32[]{:S(2)}, u32[]{:S(2)}) collective-permute-start(bf16[1,1,1536]{1,2,0:T(8,128)(2,1)S(1)} %get-tuple-element.17), channel_id=1, source_target_pairs={{0,1},{1,2},{2,3},{3,4},{4,5},{5,6},{6,7},{7,8},{8,9},{9,10},{10,1... | collective-permute-start | bytes 9224 | tf_op jit(solution)/shard_map/ppermute | solution.py:19
  420.1 20.0 %collective-permute-start.3 = (bf16[1,1,1536]{1,2,0:T(8,128)(2,1)S(1)}, bf16[1,1,1536]{1,2,0:T(8,128)(2,1)S(1)}, u32[]{:S(2)}, u32[]{:S(2)}) collective-permute-start(bf16[1,1,1536]{1,2,0:T(8,128)(2,1)S(1)} %get-tuple-element.18), channel_id=1, source_target_pairs={{1,0},{2,1},{3,2},{4,3},{5,4},{6,5},{7,6},{8,7},{9,8},{10,9},{11,1... | collective-permute-start | bytes 9224 | tf_op jit(solution)/shard_map/ppermute | solution.py:21
Sparse Core Ops, SparseCore 0:
  11.2 102.2 all-gather.2
  116.5 79.0 all-gather.4
